TPU v7x, 32 devices: a whole 2x2x4 slice. The times are simulated.
32 devices in a mesh: tok: 16 (over z, y, x), head: 2 (over core).
Axes of the slice: x: 2, y: 2, z: 4, core: 2. Of those that a mesh axis runs over, the one named last changes fastest.
Arguments:
- tokens: bfloat16 [32768, 768], P(('tok', 'head')), may hold values from -6 to 6
- cotangent: bfloat16 [32768, 768], P(('tok', 'head')), may hold values from -6 to 6
- block_source: int32 [32, 4, 2], replicated, may hold values from 0 to 1, as said below
- mask_index: int32 [32, 256], replicated, may hold values from 0 to 1023, as said below
- mask_count: int32 [32], replicated, may hold values from 51 to 256
- w_query: bfloat16 [768, 768], P(None, 'head'), may hold values from -0.21875 to 0.21875
- w_key: bfloat16 [768, 768], P(None, 'head'), may hold values from -0.21875 to 0.21875
- w_value: bfloat16 [768, 768], P(None, 'head'), may hold values from -0.21875 to 0.21875
- w_output: bfloat16 [768, 768], P('head'), may hold values from -3 to 3
- mid_gain: float32 [768], replicated, may hold values from 0.25 to 1.75
- mid_shift: float32 [768], replicated, may hold values from -3 to 3
- w_inner: bfloat16 [768, 3072], P(None, 'head'), may hold values from -0.21875 to 0.21875
- bias_inner: float32 [3072], P('head'), may hold values from -3 to 3
- w_outer: bfloat16 [3072, 768], P('head'), may hold values from -0.109375 to 0.109375
- bias_outer: float32 [768], replicated, may hold values from -3 to 3
- end_gain: float32 [768], replicated, may hold values from 0.25 to 1.75
- end_shift: float32 [768], replicated, may hold values from -3 to 3
Outputs:
- out: bfloat16 [32768, 768], P(('tok', 'head'))
- grad_tokens: float32 [32768, 768], P(('tok', 'head'))
- grad_w_query: float32 [768, 768], P(None, 'head')
- grad_w_key: float32 [768, 768], P(None, 'head')
- grad_w_value: float32 [768, 768], P(None, 'head')
- grad_w_output: float32 [768, 768], P('head')
- grad_mid_gain: float32 [768], replicated
- grad_mid_shift: float32 [768], replicated
- grad_w_inner: float32 [768, 3072], P(None, 'head')
- grad_bias_inner: float32 [3072], P('head')
- grad_w_outer: float32 [3072, 768], P('head')
- grad_bias_outer: float32 [768], replicated
- grad_end_gain: float32 [768], replicated
- grad_end_shift: float32 [768], replicated
Inputs may be any that keep to these rules, and one draw needn't show every extreme that they name: Each pair block_source[s, g] is (0, 1) or (1, 0); in every sequence at least one group has (1, 0). `mask_index`: the entries of a row are distinct positions of its sequence; only the first mask_count entries of a row are read.
All inputs are finite; a program needn't handle non-finite values.
Results may differ from a plain program's by a relative error of at most 0.015.
Values may be sent and summed in bfloat16 or wider, within the bound.
No kernel may reach another device: no remote copies, remote signals or barrier semaphores. Data moves between devices by JAX's collectives and lax.ppermute only.
A program may use at most 192 MiB of HBM per device.

v0:
```python
import jax
import jax.numpy as jnp
from jax import lax
from jax.sharding import PartitionSpec as P

HEADS = 12
HDIM = 64
GROUPS = 4
BLOCK = 512
PAIR_SEQS = 4


NORM_EPS = 1e-05


def partner(x, axis, apart):
    return lax.ppermute(x, axis, [(i, i ^ 1 << apart) for i in range(lax.axis_size(axis))])


def layer_norm(summed, gain, shift):
    center = summed - jnp.mean(summed, axis=-1, keepdims=True)
    spread = jnp.mean(center * center, axis=-1, keepdims=True)
    return center * lax.rsqrt(spread + NORM_EPS) * gain + shift


def gelu_exact(value):
    return jax.nn.gelu(value, approximate=False)


def block_scores(queries, key_block):
    scale = queries.shape[-1] ** (-0.5)
    return (
        jnp.einsum("qhd,khd->hqk", queries, key_block, preferred_element_type=jnp.float32) * scale
    )


def block_forward(operands):
    queries, key_block, value_block = operands
    scores = block_scores(queries, key_block)
    highest = jnp.max(scores, axis=-1, keepdims=True)
    powers = jnp.exp(scores - highest)
    total = jnp.sum(powers, axis=-1, keepdims=True)
    probs = (powers / total).astype(jnp.bfloat16)
    context = jnp.einsum("hqk,khd->qhd", probs, value_block, preferred_element_type=jnp.float32)
    return (context.astype(jnp.bfloat16), highest + jnp.log(total))


def block_backward(operands):
    queries, key_block, value_block, log_total, grad_context = operands
    scale = queries.shape[-1] ** (-0.5)
    probs = jnp.exp(block_scores(queries, key_block) - log_total)
    grad_values = jnp.einsum(
        "hqk,qhd->khd", probs.astype(jnp.bfloat16), grad_context, preferred_element_type=jnp.float32
    ).astype(jnp.bfloat16)
    grad_probs = jnp.einsum(
        "qhd,khd->hqk", grad_context, value_block, preferred_element_type=jnp.float32
    )
    weighted = jnp.sum(probs * grad_probs, axis=-1, keepdims=True)
    grad_scores = (probs * (grad_probs - weighted) * scale).astype(jnp.bfloat16)
    grad_queries = jnp.einsum(
        "hqk,khd->qhd", grad_scores, key_block, preferred_element_type=jnp.float32
    ).astype(jnp.bfloat16)
    grad_keys = jnp.einsum(
        "hqk,qhd->khd", grad_scores, queries, preferred_element_type=jnp.float32
    ).astype(jnp.bfloat16)
    return (grad_queries, grad_keys, grad_values)


def body(
    tokens,
    cotangent,
    block_source,
    mask_index,
    mask_count,
    w_query,
    w_key,
    w_value,
    w_output,
    mid_gain,
    mid_shift,
    w_inner,
    bias_inner,
    w_outer,
    bias_outer,
    end_gain,
    end_shift,
):
    own_rows = tokens.shape[0]
    tok_place = lax.axis_index("tok")
    head_place = lax.axis_index("head")
    half = tok_place % 2
    per_group = HEADS // GROUPS
    pair_start = tok_place // 2 * PAIR_SEQS
    full_query, full_key, full_value = (w_query, w_key, w_value)
    full_inner, full_output, full_outer, full_bias = (w_inner, w_output, w_outer, bias_inner)
    gathered = lax.all_gather(tokens, "head", axis=0, tiled=True)
    all_rows = gathered.shape[0]
    blocks = all_rows // BLOCK
    group_start = head_place * (full_query.shape[1] // HDIM // per_group)
    local_width = full_query.shape[1]
    local_heads = local_width // HDIM
    local_groups = local_heads // per_group
    w_joined = jnp.concatenate([full_query, full_key, full_value], axis=1)
    projected = jnp.dot(gathered, w_joined, preferred_element_type=jnp.float32).astype(jnp.bfloat16)
    queries = projected[:, :local_width]
    key_rows = projected[:, local_width : 2 * local_width]
    value_rows = projected[:, 2 * local_width :]
    partner_keys, partner_values = partner((key_rows, value_rows), "tok", 0)
    source = lax.dynamic_slice_in_dim(block_source, pair_start, blocks, 0)
    chosen = jnp.where(half == 0, source[:, :, 0], source[:, :, 1])
    swapped = lax.dynamic_slice_in_dim(
        (chosen != half).astype(jnp.int32), group_start, local_groups, 1
    )
    flagged = jnp.repeat(swapped, per_group * HDIM, axis=1)[:, None, :] > 0

    def by_block(array):
        return array.reshape(blocks, BLOCK, local_width)

    def by_head(array):
        return array.reshape(blocks, BLOCK, local_heads, HDIM)

    query_heads = by_head(queries)
    key_heads = by_head(jnp.where(flagged, by_block(partner_keys), by_block(key_rows)))
    value_heads = by_head(jnp.where(flagged, by_block(partner_values), by_block(value_rows)))
    context, log_total = lax.map(block_forward, (query_heads, key_heads, value_heads))
    context_rows = context.reshape(all_rows, local_width)
    branch_terms = jnp.dot(context_rows, full_output, preferred_element_type=jnp.float32)
    branch = lax.psum_scatter(branch_terms, "head", scatter_dimension=0, tiled=True)
    inputs = tokens.astype(jnp.float32)
    normed, mid_pull = jax.vjp(layer_norm, inputs + branch, mid_gain, mid_shift)
    normed_low = normed.astype(jnp.bfloat16)
    normed_all = lax.all_gather(normed_low, "head", axis=0, tiled=True)
    inner = jnp.dot(normed_all, full_inner, preferred_element_type=jnp.float32) + full_bias
    active, gelu_pull = jax.vjp(gelu_exact, inner)
    active_low = active.astype(jnp.bfloat16)
    outer_terms = jnp.dot(active_low, full_outer, preferred_element_type=jnp.float32)
    outer = lax.psum_scatter(
        outer_terms.astype(jnp.bfloat16), "head", scatter_dimension=0, tiled=True
    ).astype(jnp.float32)
    result, end_pull = jax.vjp(layer_norm, normed + outer + bias_outer, end_gain, end_shift)
    positions = lax.dynamic_slice_in_dim(mask_index, pair_start, blocks, 0)
    counts = lax.dynamic_slice_in_dim(mask_count, pair_start, blocks, 0)
    live = jnp.arange(positions.shape[1])[None, :] < counts[:, None]
    places = half * BLOCK + jnp.arange(BLOCK)
    hits = jnp.any((positions[:, :, None] == places[None, None, :]) & live[:, :, None], axis=1)
    weight_all = (1.0 + 3.0 * hits.astype(jnp.float32)).reshape(all_rows)
    row_weight = lax.dynamic_slice_in_dim(weight_all, head_place * own_rows, own_rows, 0)
    grad_result = cotangent.astype(jnp.float32) * row_weight[:, None]
    grad_second, grad_end_gain, grad_end_shift = end_pull(grad_result)
    grad_bias_outer = jnp.sum(grad_second, axis=0)
    grad_second_low = grad_second.astype(jnp.bfloat16)
    grad_outer_all = lax.all_gather(grad_second_low, "head", axis=0, tiled=True)
    grad_w_outer = jnp.einsum(
        "gf,gd->fd", active_low, grad_outer_all, preferred_element_type=jnp.float32
    )
    grad_active = jnp.einsum(
        "gd,fd->gf", grad_outer_all, full_outer, preferred_element_type=jnp.float32
    )
    grad_inner = gelu_pull(grad_active)[0]
    grad_bias_inner = jnp.sum(grad_inner, axis=0)
    grad_inner_low = grad_inner.astype(jnp.bfloat16)
    grad_w_inner = jnp.einsum(
        "gd,gf->df", normed_all, grad_inner_low, preferred_element_type=jnp.float32
    )
    back_inner = jnp.einsum(
        "gf,df->gd", grad_inner_low, full_inner, preferred_element_type=jnp.float32
    )
    grad_normed = grad_second + lax.psum_scatter(
        back_inner.astype(jnp.bfloat16), "head", scatter_dimension=0, tiled=True
    ).astype(jnp.float32)
    grad_first, grad_mid_gain, grad_mid_shift = mid_pull(grad_normed)
    grad_first_low = grad_first.astype(jnp.bfloat16)
    grad_branch_all = lax.all_gather(grad_first_low, "head", axis=0, tiled=True)
    grad_w_output = jnp.einsum(
        "gc,gd->cd", context_rows, grad_branch_all, preferred_element_type=jnp.float32
    )
    grad_context = jnp.einsum(
        "gd,cd->gc", grad_branch_all, full_output, preferred_element_type=jnp.float32
    ).astype(jnp.bfloat16)
    grad_queries, grad_keys_used, grad_values_used = lax.map(
        block_backward, (query_heads, key_heads, value_heads, log_total, by_head(grad_context))
    )
    grad_keys_used = grad_keys_used.reshape(all_rows, local_width)
    grad_values_used = grad_values_used.reshape(all_rows, local_width)
    back_keys, back_values = partner((grad_keys_used, grad_values_used), "tok", 0)
    grad_keys = jnp.where(flagged, by_block(back_keys), by_block(grad_keys_used)).reshape(
        all_rows, local_width
    )
    grad_values = jnp.where(flagged, by_block(back_values), by_block(grad_values_used)).reshape(
        all_rows, local_width
    )
    grad_joined = jnp.concatenate(
        [grad_queries.reshape(all_rows, local_width), grad_keys, grad_values], axis=1
    )
    grad_w_joined = jnp.einsum(
        "gd,gc->dc", gathered, grad_joined, preferred_element_type=jnp.float32
    )
    back_input = jnp.einsum("gc,dc->gd", grad_joined, w_joined, preferred_element_type=jnp.float32)
    grad_tokens = grad_first + lax.psum_scatter(
        back_input.astype(jnp.bfloat16), "head", scatter_dimension=0, tiled=True
    ).astype(jnp.float32)
    grad_mid_gain, grad_mid_shift, grad_end_gain, grad_end_shift, grad_bias_outer = lax.psum(
        (grad_mid_gain, grad_mid_shift, grad_end_gain, grad_end_shift, grad_bias_outer),
        ("tok", "head"),
    )
    grad_w_query = grad_w_joined[:, :local_width]
    grad_w_key = grad_w_joined[:, local_width : 2 * local_width]
    grad_w_value = grad_w_joined[:, 2 * local_width :]
    (
        grad_w_query,
        grad_w_key,
        grad_w_value,
        grad_w_output,
        grad_w_inner,
        grad_bias_inner,
        grad_w_outer,
    ) = lax.psum(
        (
            grad_w_query,
            grad_w_key,
            grad_w_value,
            grad_w_output,
            grad_w_inner,
            grad_bias_inner,
            grad_w_outer,
        ),
        "tok",
    )
    return (
        result.astype(jnp.bfloat16),
        grad_tokens,
        grad_w_query,
        grad_w_key,
        grad_w_value,
        grad_w_output,
        grad_mid_gain,
        grad_mid_shift,
        grad_w_inner,
        grad_bias_inner,
        grad_w_outer,
        grad_bias_outer,
        grad_end_gain,
        grad_end_shift,
    )


def solution(mesh):
    return jax.shard_map(
        body,
        mesh=mesh,
        in_specs=(
            P(("tok", "head"), None),
            P(("tok", "head"), None),
            P(),
            P(),
            P(),
            P(None, "head"),
            P(None, "head"),
            P(None, "head"),
            P("head", None),
            P(),
            P(),
            P(None, "head"),
            P("head"),
            P("head", None),
            P(),
            P(),
            P(),
        ),
        out_specs=(
            P(("tok", "head"), None),
            P(("tok", "head"), None),
            P(None, "head"),
            P(None, "head"),
            P(None, "head"),
            P("head", None),
            P(),
            P(),
            P(None, "head"),
            P("head"),
            P("head", None),
            P(),
            P(),
            P(),
        ),
        check_vma=False,
    )
```

profile of v0, /device:TPU:0, one launch (start us, length us, event | category | flops | bytes accessed | tf_op | source)
XLA Modules:
  0.0 1047.9 jit_solution(8665799748134953989)
XLA Ops:
  11.9 12.5 %all-gather.5.cloned.1.call-done = bf16[2048,768]{1,0:T(8,128)(2,1)} async-done(((bf16[1024,768]{1,0:T(8,128)(2,1)}), bf16[2048,768]{1,0:T(8,128)(2,1)}) %all-gather.5.cloned.1.call-update) | async-done | bytes 3145744 | tf_op jit(solution)/shard_map/all_gather | solution.py:96
  50.6 20.1 %collective-permute-done = bf16[2048,384]{0,1:T(8,128)(2,1)} collective-permute-done((bf16[2048,384]{0,1:T(8,128)(2,1)}, bf16[2048,384]{0,1:T(8,128)(2,1)}, u32[]{:S(2)}, u32[]{:S(2)}) %collective-permute-start) | collective-permute-done | bytes 1572896 | tf_op jit(solution)/shard_map/ppermute | solution.py:17
  74.5 29.2 %collective-permute-done.1 = bf16[2048,384]{0,1:T(8,128)(2,1)} collective-permute-done((bf16[2048,384]{0,1:T(8,128)(2,1)}, bf16[2048,384]{0,1:T(8,128)(2,1)}, u32[]{:S(2)}, u32[]{:S(2)}) %collective-permute-start.1) | collective-permute-done | bytes 1572896 | tf_op jit(solution)/shard_map/ppermute | solution.py:17
  115.2 27.9 %while.26 = (s32[]{:T(128)}, bf16[4,512,6,64]{1,3,2,0:T(8,128)(2,1)}, f32[4,6,512,1]{2,1,3,0:T(8,128)}, bf16[4,512,6,64]{1,3,2,0:T(8,128)(2,1)}, bf16[4,512,6,64...) while((s32[]{:T(128)}, bf16[4,512,6,64]{1,3,2,0:T(8,128)(2,1)}, ...), condition=%wide.region_3.4_spmd, body=%wide.region_0.3_spmd.sunk | while | flops 417002496 | bytes 20552268 | solution.py:125
  152.3 15.5 %reduce-scatter.5.cloned.1.call-done = f32[1024,768]{1,0:T(8,128)} async-done(((f32[2048,768]{1,0:T(8,128)}), f32[1024,768]{1,0:T(8,128)}) %reduce-scatter.5.cloned.1.call-update) | async-done | bytes 3145744 | tf_op jit(solution)/shard_map/reduce_scatter | solution.py:128
  174.0 13.4 %all-gather.7.cloned.1.call-done = bf16[2048,768]{1,0:T(8,128)(2,1)} async-done(((bf16[1024,768]{1,0:T(8,128)(2,1)}), bf16[2048,768]{1,0:T(8,128)(2,1)}) %all-gather.7.cloned.1.call-update) | async-done | bytes 3145744 | tf_op jit(solution)/shard_map/all_gather | solution.py:132
  187.4 33.8 %multiply_convert_fusion.1 = (bf16[2048,1536]{1,0:T(8,128)(2,1)S(1)}, f32[2048,1536]{1,0:T(8,128)}, f32[2048,1536]{1,0:T(8,128)}) fusion(f32[1536]{0:T(1024)S(1)} %copy-done.39, bf16[2048,768]{1,0:T(8,128)(2,1)} %all-gather.7.cloned.1.call-done, bf16[768,1536]{1,0:T(8,128)(2,1)S(1)} %copy-done), kind=kOutput, calls=%fused_computation.73 | convolution fusion | flops 5039456256 | bytes 36968448 | tf_op jit(solution)/shard_map/dot_general | solution.py:133
  256.0 12.9 %all-gather.9.cloned.1.call-done = bf16[2048,768]{1,0:T(8,128)(2,1)} async-done(((bf16[1024,768]{1,0:T(8,128)(2,1)}), bf16[2048,768]{1,0:T(8,128)(2,1)}) %all-gather.9.cloned.1.call-update) | async-done | bytes 3145744 | tf_op jit(solution)/shard_map/all_gather | solution.py:152
  269.0 16.8 %fusion.120 = (f32[1536]{0:T(1024)S(1)}, bf16[2048,1536]{1,0:T(8,128)(2,1)S(1)}) fusion(f32[2048,1536]{1,0:T(8,128)} %get-tuple-element.272, bf16[2048,768]{1,0:T(8,128)(2,1)} %all-gather.9.cloned.1.call-done, bf16[1536,768]{1,0:T(8,128)(2,1)} %param.34, f32[2048,1536]{1,0:T(8,128)} %get-tuple-element.290, f32[1536]{0:T(1024)S(1)} %copy-done.39), kind=kOutput, calls=%fused_computation.154 | convolution fusion | flops 4882168320 | bytes 36974592 | tf_op jit(solution)/shard_map/gd,fd->gf/dot_general | solution.py:156
  317.9 13.2 %all-gather.11.cloned.1.call-done = bf16[2048,768]{1,0:T(8,128)(2,1)} async-done(((bf16[1024,768]{1,0:T(8,128)(2,1)}), bf16[2048,768]{1,0:T(8,128)(2,1)}) %all-gather.11.cloned.1.call-update) | async-done | bytes 3145744 | tf_op jit(solution)/shard_map/all_gather | solution.py:173
  349.3 159.1 %while.27 = (s32[]{:T(128)}, bf16[4,512,6,64]{1,3,2,0:T(8,128)(2,1)}, bf16[4,512,6,64]{1,3,2,0:T(8,128)(2,1)}, bf16[4,512,6,64]{1,3,2,0:T(8,128)(2,1)}, bf16[4,5...) while((s32[]{:T(128)}, ...), condition=%wide.region_18.19_spmd, body=%wide.region_16.18_spmd.sunk | while | flops 1040260096 | bytes 73245800 | solution.py:180
  359.5 12.4 %fusion.180 = bf16[4,512,6,64]{1,3,2,0:T(8,128)(2,1)} fusion(bf16[4,512,6,64]{1,3,2,0:T(8,128)(2,1)} %get-tuple-element.424, s32[]{:T(128)} %get-tuple-element.422, f32[6,512,512]{1,2,0:T(8,128)} %fusion.177, f32[6,512,512]{1,2,0:T(8,128)} %fusion.178, f32[6,512]{1,0:T(8,128)S(1)} %dynamic-slice_bitcast_fusion.2, ...), kind=kOutput, calls=%fused_computation.38.clone.1 | convolution fusion | flops 215682560 | bytes 25986048 | tf_op jit(solution)/shard_map/while/body/eval_jaxpr/hqk,qhd->khd/dot_general | solution.py:63
  371.8 12.3 %fusion.179 = bf16[4,512,6,64]{1,3,2,0:T(8,128)(2,1)} fusion(bf16[4,512,6,64]{1,3,2,0:T(8,128)(2,1)} %get-tuple-element.423, s32[]{:T(128)} %get-tuple-element.422, f32[6,512,512]{1,2,0:T(8,128)} %fusion.177, f32[6,512,512]{1,2,0:T(8,128)} %fusion.178, f32[6,512]{1,0:T(8,128)S(1)} %dynamic-slice_bitcast_fusion.2, ...), kind=kOutput, calls=%fused_computation.40.clone.1 | convolution fusion | flops 215682560 | bytes 25986048 | tf_op jit(solution)/shard_map/while/body/eval_jaxpr/hqk,khd->qhd/dot_general | solution.py:60
  399.2 12.3 %fusion.180 = bf16[4,512,6,64]{1,3,2,0:T(8,128)(2,1)} fusion(bf16[4,512,6,64]{1,3,2,0:T(8,128)(2,1)} %get-tuple-element.424, s32[]{:T(128)} %get-tuple-element.422, f32[6,512,512]{1,2,0:T(8,128)} %fusion.177, f32[6,512,512]{1,2,0:T(8,128)} %fusion.178, f32[6,512]{1,0:T(8,128)S(1)} %dynamic-slice_bitcast_fusion.2, ...), kind=kOutput, calls=%fused_computation.38.clone.1 | convolution fusion | flops 215682560 | bytes 25986048 | tf_op jit(solution)/shard_map/while/body/eval_jaxpr/hqk,qhd->khd/dot_general | solution.py:63
  411.6 12.3 %fusion.179 = bf16[4,512,6,64]{1,3,2,0:T(8,128)(2,1)} fusion(bf16[4,512,6,64]{1,3,2,0:T(8,128)(2,1)} %get-tuple-element.423, s32[]{:T(128)} %get-tuple-element.422, f32[6,512,512]{1,2,0:T(8,128)} %fusion.177, f32[6,512,512]{1,2,0:T(8,128)} %fusion.178, f32[6,512]{1,0:T(8,128)S(1)} %dynamic-slice_bitcast_fusion.2, ...), kind=kOutput, calls=%fused_computation.40.clone.1 | convolution fusion | flops 215682560 | bytes 25986048 | tf_op jit(solution)/shard_map/while/body/eval_jaxpr/hqk,khd->qhd/dot_general | solution.py:60
  439.0 12.4 %fusion.180 = bf16[4,512,6,64]{1,3,2,0:T(8,128)(2,1)} fusion(bf16[4,512,6,64]{1,3,2,0:T(8,128)(2,1)} %get-tuple-element.424, s32[]{:T(128)} %get-tuple-element.422, f32[6,512,512]{1,2,0:T(8,128)} %fusion.177, f32[6,512,512]{1,2,0:T(8,128)} %fusion.178, f32[6,512]{1,0:T(8,128)S(1)} %dynamic-slice_bitcast_fusion.2, ...), kind=kOutput, calls=%fused_computation.38.clone.1 | convolution fusion | flops 215682560 | bytes 25986048 | tf_op jit(solution)/shard_map/while/body/eval_jaxpr/hqk,qhd->khd/dot_general | solution.py:63
  451.3 12.3 %fusion.179 = bf16[4,512,6,64]{1,3,2,0:T(8,128)(2,1)} fusion(bf16[4,512,6,64]{1,3,2,0:T(8,128)(2,1)} %get-tuple-element.423, s32[]{:T(128)} %get-tuple-element.422, f32[6,512,512]{1,2,0:T(8,128)} %fusion.177, f32[6,512,512]{1,2,0:T(8,128)} %fusion.178, f32[6,512]{1,0:T(8,128)S(1)} %dynamic-slice_bitcast_fusion.2, ...), kind=kOutput, calls=%fused_computation.40.clone.1 | convolution fusion | flops 215682560 | bytes 25986048 | tf_op jit(solution)/shard_map/while/body/eval_jaxpr/hqk,khd->qhd/dot_general | solution.py:60
  478.7 12.3 %fusion.180 = bf16[4,512,6,64]{1,3,2,0:T(8,128)(2,1)} fusion(bf16[4,512,6,64]{1,3,2,0:T(8,128)(2,1)} %get-tuple-element.424, s32[]{:T(128)} %get-tuple-element.422, f32[6,512,512]{1,2,0:T(8,128)} %fusion.177, f32[6,512,512]{1,2,0:T(8,128)} %fusion.178, f32[6,512]{1,0:T(8,128)S(1)} %dynamic-slice_bitcast_fusion.2, ...), kind=kOutput, calls=%fused_computation.38.clone.1 | convolution fusion | flops 215682560 | bytes 25986048 | tf_op jit(solution)/shard_map/while/body/eval_jaxpr/hqk,qhd->khd/dot_general | solution.py:63
  491.0 12.3 %fusion.179 = bf16[4,512,6,64]{1,3,2,0:T(8,128)(2,1)} fusion(bf16[4,512,6,64]{1,3,2,0:T(8,128)(2,1)} %get-tuple-element.423, s32[]{:T(128)} %get-tuple-element.422, f32[6,512,512]{1,2,0:T(8,128)} %fusion.177, f32[6,512,512]{1,2,0:T(8,128)} %fusion.178, f32[6,512]{1,0:T(8,128)S(1)} %dynamic-slice_bitcast_fusion.2, ...), kind=kOutput, calls=%fused_computation.40.clone.1 | convolution fusion | flops 215682560 | bytes 25986048 | tf_op jit(solution)/shard_map/while/body/eval_jaxpr/hqk,khd->qhd/dot_general | solution.py:60
  518.2 30.7 %collective-permute-done.2 = bf16[2048,384]{0,1:T(8,128)(2,1)S(1)} collective-permute-done((bf16[2048,384]{0,1:T(8,128)(2,1)S(1)}, bf16[2048,384]{0,1:T(8,128)(2,1)S(1)}, u32[]{:S(2)}, u32[]{:S(2)}) %collective-permute-start.2) | collective-permute-done | bytes 1572896 | tf_op jit(solution)/shard_map/ppermute | solution.py:17
  548.9 33.1 %collective-permute-done.3 = bf16[2048,384]{0,1:T(8,128)(2,1)S(1)} collective-permute-done((bf16[2048,384]{0,1:T(8,128)(2,1)S(1)}, bf16[2048,384]{0,1:T(8,128)(2,1)S(1)}, u32[]{:S(2)}, u32[]{:S(2)}) %collective-permute-start.3) | collective-permute-done | bytes 1572896 | tf_op jit(solution)/shard_map/ppermute | solution.py:17
  620.9 45.6 %psum.91 = f32[1536]{0:T(1024)} all-reduce(f32[1536]{0:T(1024)S(1)} %get-tuple-element.291), channel_id=1, replica_groups=mesh['tok'=16,'head'=2] {'tok'}, use_global_device_ids=true, to_apply=%region_30.31 | all-reduce | flops 1536 | bytes 12288 | tf_op jit(solution)/shard_map/psum | solution.py:217
  666.5 41.5 %all-reduce = (f32[768]{0:T(1024)}, f32[768]{0:T(1024)}, f32[768]{0:T(1024)}, f32[768]{0:T(1024)}, f32[768]{0:T(1024)}) all-reduce(f32[768]{0:T(1024)S(1)} %get-tuple-element.217, f32[768]{0:T(1024)S(1)} %get-tuple-element.221, f32[768]{0:T(1024)S(1)} %get-tuple-element.222, ...), channel_id=1, replica_groups=mesh['tok'=16,'head'=2] {'tok','head'}, use_global_device_ids=true, to_apply=%region_25.26 | all-reduce | flops 3840 | bytes 30720 | tf_op jit(solution)/shard_map/psum | solution.py:202
  712.7 311.4 %all-reduce.4.cloned.1.call-done = (f32[768,384]{0,1:T(8,128)}, f32[768,384]{0,1:T(8,128)}, f32[768,384]{0,1:T(8,128)}, f32[384,768]{1,0:T(8,128)}, f32[768,1536]{1,0:T(8,128)}, /*index=5*/f32[1536,768]{1,0:T(8,128)}) async-done(((f32[768,384]{0,1:T(8,128)}, f32[768,384]{0,1:T(8,128)}, f32[768,384]{0,1:T(8,128)}, f32[384,768]{1,0:T(8,128)}, f32[768,1536]{1,0:T(8,128)}, /*index=5*/f32[1536,768]{1,0:T(8,128)}), ...) | async-done | bytes 14155792 | tf_op jit(solution)/shard_map/psum | solution.py:217
  (230 shorter events, 304.4 us)
Async XLA Ops:
  7.2 180.2 %copy-start = (bf16[768,1536]{1,0:T(8,128)(2,1)S(1)}, bf16[768,1536]{1,0:T(8,128)(2,1)}, u32[]{:S(2)}) copy-start(bf16[768,1536]{1,0:T(8,128)(2,1)} %param.32) | copy-start | bytes 7077892
  7.2 17.2 %all-gather.5.cloned.1.call-start = ((), (), s32[]{:S(2)}) async-start(), calls=%async_computation.4 | async-start | bytes 4718592 | tf_op jit(solution)/shard_map/all_gather | solution.py:96
  8.0 159.9 %reduce-scatter.5.cloned.1.call-start = ((), (), s32[]{:S(2)}) async-start(), calls=%async_computation.5 | async-start | bytes 9437184 | tf_op jit(solution)/shard_map/reduce_scatter | solution.py:128
  33.2 37.5 %collective-permute-start = (bf16[2048,384]{0,1:T(8,128)(2,1)}, bf16[2048,384]{0,1:T(8,128)(2,1)}, u32[]{:S(2)}, u32[]{:S(2)}) collective-permute-start(bf16[2048,384]{0,1:T(8,128)(2,1)} %get-tuple-element.279), channel_id=1, source_target_pairs={{0,2},{2,0},{4,6},{6,4},{8,10},{10,8},{12,14},{14,12},{16,18},{18,... | collective-permute-start | bytes 4718600 | tf_op jit(solution)/shard_map/ppermute | solution.py:17
  34.9 68.9 %collective-permute-start.1 = (bf16[2048,384]{0,1:T(8,128)(2,1)}, bf16[2048,384]{0,1:T(8,128)(2,1)}, u32[]{:S(2)}, u32[]{:S(2)}) collective-permute-start(bf16[2048,384]{0,1:T(8,128)(2,1)} %get-tuple-element.277), channel_id=1, source_target_pairs={{0,2},{2,0},{4,6},{6,4},{8,10},{10,8},{12,14},{14,12},{16,18},{18,... | collective-permute-start | bytes 4718600 | tf_op jit(solution)/shard_map/ppermute | solution.py:17
  152.0 35.4 %all-gather.7.cloned.1.call-start = ((), (), s32[]{:S(2)}) async-start(), calls=%async_computation.6 | async-start | bytes 4718592 | tf_op jit(solution)/shard_map/all_gather | solution.py:132
  172.2 15.2 %copy-start.39 = (f32[1536]{0:T(1024)S(1)}, f32[1536]{0:T(1024)}, u32[]{:S(2)}) copy-start(f32[1536]{0:T(1024)} %param.33) | copy-start | bytes 18436
  174.0 68.6 %reduce-scatter.7.cloned.1.call-start = ((), (), s32[]{:S(2)}) async-start(), calls=%async_computation.7 | async-start | bytes 4718592 | tf_op jit(solution)/shard_map/reduce_scatter | solution.py:137
  187.4 36.5 %copy-start.38 = (bf16[1536,768]{1,0:T(8,128)(2,1)S(1)}, bf16[1536,768]{1,0:T(8,128)(2,1)}, u32[]{:S(2)}) copy-start(bf16[1536,768]{1,0:T(8,128)(2,1)} %param.34) | copy-start | bytes 7077892
  230.3 12.2 %copy-start.31 = (f32[768]{0:T(1024)S(1)}, f32[768]{0:T(1024)}, u32[]{:S(2)}) copy-start(f32[768]{0:T(1024)} %param.35) | copy-start | bytes 9220
  230.3 38.6 %all-gather.9.cloned.1.call-start = ((), (), s32[]{:S(2)}) async-start(), calls=%async_computation.8 | async-start | bytes 4718592 | tf_op jit(solution)/shard_map/all_gather | solution.py:152
  255.5 51.7 %reduce-scatter.9.cloned.1.call-start = ((), (), s32[]{:S(2)}) async-start(), calls=%async_computation.9 | async-start | bytes 4718592 | tf_op jit(solution)/shard_map/reduce_scatter | solution.py:168
  294.9 16.6 %copy-start.25 = (f32[1024]{0:T(1024)S(1)}, f32[1024]{0:T(1024)}, u32[]{:S(2)}) copy-start(f32[1024]{0:T(1024)} %copy-done.24) | copy-start | bytes 12292
  295.0 36.1 %all-gather.11.cloned.1.call-start = ((), (), s32[]{:S(2)}) async-start(), calls=%async_computation.10 | async-start | bytes 4718592 | tf_op jit(solution)/shard_map/all_gather | solution.py:173
  316.3 14.9 %copy-start.20 = (bf16[384,768]{1,0:T(8,128)(2,1)S(1)}, bf16[384,768]{1,0:T(8,128)(2,1)}, u32[]{:S(2)}) copy-start(bf16[384,768]{1,0:T(8,128)(2,1)} %param.29) | copy-start | bytes 1769476
  317.7 390.3 %reduce-scatter.11.cloned.1.call-start = ((), (), s32[]{:S(2)}) async-start(), calls=%async_computation.11 | async-start | bytes 4718592 | tf_op jit(solution)/shard_map/reduce_scatter | solution.py:199
  511.6 37.3 %collective-permute-start.2 = (bf16[2048,384]{0,1:T(8,128)(2,1)S(1)}, bf16[2048,384]{0,1:T(8,128)(2,1)S(1)}, u32[]{:S(2)}, u32[]{:S(2)}) collective-permute-start(bf16[2048,384]{0,1:T(8,128)(2,1)S(1)} %bitcast.167), channel_id=1, source_target_pairs={{0,2},{2,0},{4,6},{6,4},{8,10},{10,8},{12,14},{14,12},{16,18},{18,... | collective-permute-start | bytes 4718600 | tf_op jit(solution)/shard_map/ppermute | solution.py:17
  515.1 66.9 %collective-permute-start.3 = (bf16[2048,384]{0,1:T(8,128)(2,1)S(1)}, bf16[2048,384]{0,1:T(8,128)(2,1)S(1)}, u32[]{:S(2)}, u32[]{:S(2)}) collective-permute-start(bf16[2048,384]{0,1:T(8,128)(2,1)S(1)} %bitcast.169), channel_id=1, source_target_pairs={{0,2},{2,0},{4,6},{6,4},{8,10},{10,8},{12,14},{14,12},{16,18},{18,... | collective-permute-start | bytes 4718600 | tf_op jit(solution)/shard_map/ppermute | solution.py:17
  518.2 64.2 %copy-start.16 = (bf16[48,8,4,512]{3,1,2,0:T(8,128)(2,1)}, bf16[48,8,4,512]{3,1,2,0:T(8,128)(2,1)S(1)}, u32[]{:S(2)}) copy-start(bf16[48,8,4,512]{3,1,2,0:T(8,128)(2,1)S(1)} %copy.131) | copy-start | bytes 4718596
  591.3 432.8 %all-reduce.4.cloned.1.call-start = ((), (), s32[]{:S(2)}) async-start(), calls=%async_computation.12 | async-start | bytes 28311552 | tf_op jit(solution)/shard_map/psum | solution.py:217
  601.3 10.0 copy-start.7
  601.3 10.0 copy-start.37
  620.8 45.6 %copy-start.28 = (f32[768]{0:T(1024)S(1)}, f32[768]{0:T(1024)}, u32[]{:S(2)}) copy-start(f32[768]{0:T(1024)} %get-tuple-element.219) | copy-start | bytes 9220
  620.8 45.6 %copy-start.29 = (f32[768]{0:T(1024)S(1)}, f32[768]{0:T(1024)}, u32[]{:S(2)}) copy-start(f32[768]{0:T(1024)} %get-tuple-element.223) | copy-start | bytes 9220
  (34 other events, 106.4 us)
Sparse Core Ops, SparseCore 0:
  9.6 14.8 all-gather.4
  152.1 15.6 reduce-scatter.4
  174.1 13.2 all-gather.6
  230.5 12.0 reduce-scatter.6
  255.6 13.2 all-gather.8
  295.1 12.0 reduce-scatter.8
  317.8 13.2 all-gather.10
  591.4 12.0 reduce-scatter.10
  621.0 403.0 all-reduce.3
where the time goes:
time: 1050 us
  waiting for transfers between devices  515 us (49%)
  matrix products  290 us (28%)
  local copies, waits for them, and re-layouts  93.7 us (9%)
  blocking collectives  87.1 us (8%)
  other arithmetic  41.5 us (4%)
  between operations  14.8 us (1%)
    psum x1, waiting for transfers between devices, body(): lax.psum((grad_w_query, grad_w_key, grad_w_value, grad_w_output, grad_w_i...  311 us
    ppermute x4, waiting for transfers between devices, partner(): lax.ppermute(x, axis, [(i, i ^ 1 << apart) for i in range(lax.axis_size(a...  113 us
    dot_general x4, matrix products, block_backward(): jnp.einsum('hqk,qhd->khd', grad_scores, queries, preferred_element_type=j...  49.4 us
    dot_general x4, matrix products, block_backward(): jnp.einsum('hqk,khd->qhd', grad_scores, key_block, preferred_element_type...  49.2 us
    psum x1, blocking collectives, body(): lax.psum((grad_w_query, grad_w_key, grad_w_value, grad_w_output, grad_w_i...  45.6 us
    psum x1, blocking collectives, body(): lax.psum((grad_mid_gain, grad_mid_shift, grad_end_gain, grad_end_shift, g...  41.5 us
    unnamed x104, local copies, waits for them, and re-layouts  39.3 us
    dot_general x1, matrix products, body(): jnp.dot(normed_all, full_inner, preferred_element_type=jnp.float32)  33.8 us
  transfers between devices with their start and end apart: 13, of which 12 were waited for; matrix products, arithmetic and copies ran while one was open for 6% of the time, Pallas kernels for 0%

commit v1 on v0

v1 whole, which is shorter than its diff:
```python
import functools

import jax
import jax.numpy as jnp
from jax import lax
from jax.experimental import pallas as pl
from jax.experimental.pallas import tpu as pltpu
from jax.sharding import PartitionSpec as P

HEADS = 12
HDIM = 64
GROUPS = 4
BLOCK = 512
PAIR_SEQS = 4
LANES = 128

NORM_EPS = 1e-05
LOG2E = 1.4426950408889634
BF16 = jnp.bfloat16
F32 = jnp.float32


def swap_bit(x, axis, bit):
    return lax.ppermute(x, axis, [(i, i ^ 1 << bit) for i in range(lax.axis_size(axis))])


def dot(a, b, dims=((1,), (0,))):
    return lax.dot_general(a, b, (dims, ((), ())), preferred_element_type=F32)


NT = ((1,), (1,))
TN = ((0,), (0,))


def head_lanes(first):
    lane = lax.broadcasted_iota(jnp.int32, (1, LANES), 1)
    return (lane < HDIM) if first else (lane >= HDIM)


def attend_kernel(swap_ref, qkv_ref, ctx_ref, lse_ref):
    swap = swap_ref[...] > 0
    keys = [qkv_ref[i * BLOCK : (i + 1) * BLOCK, LANES : 2 * LANES] for i in (0, 1)]
    values = [qkv_ref[i * BLOCK : (i + 1) * BLOCK, 2 * LANES :] for i in (0, 1)]
    scale = LOG2E * HDIM**-0.5
    ones = jnp.ones((16, BLOCK), BF16)
    for i in (0, 1):
        rows = slice(i * BLOCK, (i + 1) * BLOCK)
        q = qkv_ref[rows, :LANES]
        k = jnp.where(swap, keys[1 - i], keys[i])
        v_t = jnp.where(swap, values[1 - i], values[i]).T
        parts = []
        for n in (0, 1):
            q_n = jnp.where(head_lanes(n == 0), q, jnp.zeros_like(q))
            s = dot(k, q_n, NT)
            top = jnp.max(s, axis=0, keepdims=True)
            p = jnp.exp2((s - top) * scale).astype(BF16)
            v_n = jnp.concatenate([v_t[n * HDIM : (n + 1) * HDIM], ones], axis=0)
            acc = dot(v_n, p)
            total = acc[HDIM : HDIM + 1]
            parts.append(acc[:HDIM] / total)
            lse_ref[0, n : n + 1, rows] = top * scale + jnp.log2(total)
        ctx_ref[rows, :] = jnp.concatenate(parts, axis=0).T.astype(BF16)


def attend_back_kernel(swap_ref, qkv_ref, ctx_ref, dctx_ref, lse_ref, dqkv_ref):
    swap = swap_ref[...] > 0
    keys = [qkv_ref[i * BLOCK : (i + 1) * BLOCK, LANES : 2 * LANES] for i in (0, 1)]
    values = [qkv_ref[i * BLOCK : (i + 1) * BLOCK, 2 * LANES :] for i in (0, 1)]
    scale = LOG2E * HDIM**-0.5
    found = []
    for i in (0, 1):
        rows = slice(i * BLOCK, (i + 1) * BLOCK)
        q = qkv_ref[rows, :LANES]
        k = jnp.where(swap, keys[1 - i], keys[i])
        v = jnp.where(swap, values[1 - i], values[i])
        k_t = k.T
        dctx = dctx_ref[rows, :]
        prod_t = (dctx.astype(F32) * ctx_ref[rows, :].astype(F32)).T
        dq_t = []
        dk = dv = None
        for n in (0, 1):
            own = head_lanes(n == 0)
            cut = slice(n * HDIM, (n + 1) * HDIM)
            q_n = jnp.where(own, q, jnp.zeros_like(q))
            d_n = jnp.where(own, dctx, jnp.zeros_like(dctx))
            p = jnp.exp2(dot(k, q_n, NT) * scale - lse_ref[0, n : n + 1, rows])
            inner = jnp.sum(prod_t[cut], axis=0, keepdims=True)
            ds = (p * (dot(v, d_n, NT) - inner)).astype(BF16)
            dv_n = dot(p.astype(BF16), d_n)
            dk_n = dot(ds, q_n)
            dv = dv_n if dv is None else dv + dv_n
            dk = dk_n if dk is None else dk + dk_n
            dq_t.append(dot(k_t[cut], ds))
        dq = jnp.concatenate(dq_t, axis=0).T
        dqkv_ref[rows, :LANES] = (dq * HDIM**-0.5).astype(BF16)
        found.append(((dk * HDIM**-0.5).astype(BF16), dv.astype(BF16)))
    for i in (0, 1):
        rows = slice(i * BLOCK, (i + 1) * BLOCK)
        for at in (0, 1):
            dqkv_ref[rows, (at + 1) * LANES : (at + 2) * LANES] = jnp.where(
                swap, found[1 - i][at], found[i][at]
            )


def attention(swap_lanes, qkv):
    rows = qkv.shape[0]
    pairs = qkv.shape[1] // (3 * LANES)
    units = 4 * pairs
    return pl.pallas_call(
        attend_kernel,
        grid=(pairs,),
        in_specs=[
            pl.BlockSpec((1, LANES), lambda p: (0, p)),
            pl.BlockSpec((rows, 3 * LANES), lambda p: (0, p)),
        ],
        out_specs=[
            pl.BlockSpec((rows, LANES), lambda p: (0, p)),
            pl.BlockSpec((1, 2, rows), lambda p: (p, 0, 0)),
        ],
        out_shape=[
            jax.ShapeDtypeStruct((rows, pairs * LANES), BF16),
            jax.ShapeDtypeStruct((pairs, 2, rows), F32),
        ],
        compiler_params=pltpu.CompilerParams(vmem_limit_bytes=48 * 1024 * 1024),
        cost_estimate=pl.CostEstimate(
            flops=units * 4 * BLOCK * BLOCK * 256,
            bytes_accessed=rows * pairs * LANES * 8,
            transcendentals=units * BLOCK * BLOCK,
        ),
        name="attention_forward",
    )(swap_lanes, qkv)


def attention_back(swap_lanes, qkv, ctx, dctx, lse):
    rows = qkv.shape[0]
    pairs = qkv.shape[1] // (3 * LANES)
    units = 4 * pairs
    return pl.pallas_call(
        attend_back_kernel,
        grid=(pairs,),
        in_specs=[
            pl.BlockSpec((1, LANES), lambda p: (0, p)),
            pl.BlockSpec((rows, 3 * LANES), lambda p: (0, p)),
            pl.BlockSpec((rows, LANES), lambda p: (0, p)),
            pl.BlockSpec((rows, LANES), lambda p: (0, p)),
            pl.BlockSpec((1, 2, rows), lambda p: (p, 0, 0)),
        ],
        out_specs=pl.BlockSpec((rows, 3 * LANES), lambda p: (0, p)),
        out_shape=jax.ShapeDtypeStruct(qkv.shape, BF16),
        compiler_params=pltpu.CompilerParams(vmem_limit_bytes=48 * 1024 * 1024),
        cost_estimate=pl.CostEstimate(
            flops=units * 10 * BLOCK * BLOCK * 256,
            bytes_accessed=rows * pairs * LANES * 16,
            transcendentals=units * BLOCK * BLOCK,
        ),
        name="attention_backward",
    )(swap_lanes, qkv, ctx, dctx, lse)


def normalize(summed):
    center = summed - jnp.mean(summed, axis=-1, keepdims=True)
    rate = lax.rsqrt(jnp.mean(center * center, axis=-1, keepdims=True) + NORM_EPS)
    return center * rate, rate


def norm_back(grad, normed, rate, gain):
    scaled = grad * gain
    return rate * (
        scaled
        - jnp.mean(scaled, axis=-1, keepdims=True)
        - normed * jnp.mean(scaled * normed, axis=-1, keepdims=True)
    )


def gelu_parts(u):
    size = jnp.abs(u)
    bell = jnp.exp2(u * u * (-0.5 * LOG2E))
    t = 1.0 / (1.0 + (0.3275911 * 0.5**0.5) * size)
    poly = t * (
        0.5 * 0.254829592
        + t
        * (
            0.5 * -0.284496736
            + t * (0.5 * 1.421413741 + t * (0.5 * -1.453152027 + t * (0.5 * 1.061405429)))
        )
    )
    tail = poly * bell
    phi = jnp.where(u > 0, 1.0 - tail, tail)
    return u * phi, phi + u * (bell * 0.3989422804014327)


def halves(x, place):
    rows = x.shape[0] // 2
    return (
        lax.dynamic_slice_in_dim(x, place * rows, rows, 0),
        lax.dynamic_slice_in_dim(x, (1 - place) * rows, rows, 0),
    )


def joined(mine, other, place):
    return jnp.where(
        place == 0,
        jnp.concatenate([mine, other], axis=0),
        jnp.concatenate([other, mine], axis=0),
    )


def add_low(a, b):
    return (a.astype(F32) + b.astype(F32)).astype(BF16)


def tok_sum(first, second):
    size = lax.axis_size("tok")
    place = lax.axis_index("tok")
    bits = size.bit_length() - 1

    def at(bit):
        return place >> bit & 1

    def scatter(x, bit):
        mine, other = halves(x, at(bit))
        return add_low(mine, swap_bit(other, "tok", bit))

    def gather(x, bit):
        return joined(x, swap_bit(x, "tok", bit), at(bit))

    a, b = first, second
    a, b = scatter(a, 0), scatter(b, 1)
    a, b = scatter(a, 1), scatter(b, 0)
    rows = a.shape[0]
    for bit in range(2, bits):
        mine_a, other_a = halves(a, at(bit))
        mine_b, other_b = halves(b, at(bit))
        got = swap_bit(jnp.concatenate([other_a, other_b], axis=0), "tok", bit)
        cut = mine_a.shape[0]
        a, b = add_low(mine_a, got[:cut]), add_low(mine_b, got[cut:])
    for bit in reversed(range(2, bits)):
        cut = a.shape[0]
        got = swap_bit(jnp.concatenate([a, b], axis=0), "tok", bit)
        a, b = joined(a, got[:cut], at(bit)), joined(b, got[cut:], at(bit))
    a, b = gather(a, 1), gather(b, 0)
    a, b = gather(a, 0), gather(b, 1)
    return a, b


def body(
    tokens,
    cotangent,
    block_source,
    mask_index,
    mask_count,
    w_query,
    w_key,
    w_value,
    w_output,
    mid_gain,
    mid_shift,
    w_inner,
    bias_inner,
    w_outer,
    bias_outer,
    end_gain,
    end_shift,
):
    tok_place = lax.axis_index("tok")
    head_place = lax.axis_index("head")
    half = tok_place % 2
    width = tokens.shape[1]

    def mate(x):
        return swap_bit(x, "head", 0)

    kept, given = halves(tokens, half)
    x = jnp.concatenate([kept, swap_bit(given, "tok", 0)], axis=0)
    cot_kept, cot_given = halves(cotangent, half)
    cot = jnp.concatenate([cot_kept, swap_bit(cot_given, "tok", 0)], axis=0)

    local_pairs = w_query.shape[1] // LANES
    w_own = jnp.concatenate(
        [
            w[:, p * LANES : (p + 1) * LANES]
            for p in range(local_pairs)
            for w in (w_query, w_key, w_value)
        ],
        axis=1,
    )
    w_qkv = jnp.concatenate([w_own, mate(w_own)], axis=1)
    w_out = jnp.concatenate([w_output, mate(w_output)], axis=0)
    w_in = jnp.concatenate([w_inner, mate(w_inner)], axis=1)
    b_in = jnp.concatenate([bias_inner, mate(bias_inner)], axis=0)
    w_down = jnp.concatenate([w_outer, mate(w_outer)], axis=0)
    hidden = w_inner.shape[1]

    sequence = tok_place // 2 * PAIR_SEQS + 2 * head_place + half
    source = lax.dynamic_slice_in_dim(block_source, sequence, 1, 0)[0, :, 0]
    per_half = GROUPS // 2
    flags = jnp.concatenate(
        [
            lax.dynamic_slice_in_dim(source, head_place * per_half, per_half, 0),
            lax.dynamic_slice_in_dim(source, (1 - head_place) * per_half, per_half, 0),
        ]
    )
    swap_lanes = jnp.repeat(flags, HEADS // GROUPS * HDIM)[None, :]
    positions = lax.dynamic_slice_in_dim(mask_index, sequence, 1, 0)[0]
    count = lax.dynamic_slice_in_dim(mask_count, sequence, 1, 0)[0]
    within = jnp.arange(BLOCK)
    places = jnp.concatenate([half * BLOCK + within, (1 - half) * BLOCK + within])
    live = jnp.arange(positions.shape[0]) < count
    hits = jnp.any((positions[None, :] == places[:, None]) & live[None, :], axis=1)
    weight = 1.0 + 3.0 * hits.astype(F32)

    qkv = dot(x, w_qkv).astype(BF16)
    ctx, lse = attention(swap_lanes, qkv)
    mid_n, mid_rate = normalize(x.astype(F32) + dot(ctx, w_out))
    h1 = mid_n * mid_gain + mid_shift
    h1_low = h1.astype(BF16)
    active, slope = gelu_parts(dot(h1_low, w_in) + b_in)
    active = active.astype(BF16)
    slope = slope.astype(BF16)
    end_n, end_rate = normalize(h1 + dot(active, w_down) + bias_outer)
    out = (end_n * end_gain + end_shift).astype(BF16)
    out = joined(out[:BLOCK], swap_bit(out[BLOCK:], "tok", 0), half)

    d_y = cot.astype(F32) * weight[:, None]
    grad_end_shift = jnp.sum(d_y, axis=0)
    grad_end_gain = jnp.sum(d_y * end_n, axis=0)
    d_s2 = norm_back(d_y, end_n, end_rate, end_gain)
    grad_bias_outer = jnp.sum(d_s2, axis=0)
    d_f = d_s2.astype(BF16)

    def down_grad(rows):
        return dot(active[:, rows], d_f, TN)

    got = mate(down_grad(slice(hidden, 2 * hidden)).astype(BF16))
    g_down = (down_grad(slice(0, hidden)) + got.astype(F32)).astype(BF16)

    d_u = dot(d_f, w_down, NT) * slope.astype(F32)
    grad_b_in = jnp.sum(d_u, axis=0)
    d_u = d_u.astype(BF16)

    def inner_grad(cols):
        return dot(h1_low, d_u[:, cols], TN)

    got = mate(inner_grad(slice(hidden, 2 * hidden)).astype(BF16))
    g_in = (inner_grad(slice(0, hidden)) + got.astype(F32)).astype(BF16)

    d_h1 = d_s2 + dot(d_u, w_in, NT)
    grad_mid_shift = jnp.sum(d_h1, axis=0)
    grad_mid_gain = jnp.sum(d_h1 * mid_n, axis=0)
    d_s1 = norm_back(d_h1, mid_n, mid_rate, mid_gain)
    d_a = d_s1.astype(BF16)
    own_out = w_output.shape[0]
    got = mate(dot(ctx[:, own_out:], d_a, TN).astype(BF16))
    g_out = (dot(ctx[:, :own_out], d_a, TN) + got.astype(F32)).astype(BF16)
    d_ctx = dot(d_a, w_out, NT).astype(BF16)

    d_qkv = attention_back(swap_lanes, qkv, ctx, d_ctx, lse)
    own_qkv = w_own.shape[1]
    got = mate(dot(x, d_qkv[:, own_qkv:], TN).astype(BF16))
    g_qkv = (dot(x, d_qkv[:, :own_qkv], TN) + got.astype(F32)).astype(BF16)
    d_x = d_s1 + dot(d_qkv, w_qkv, NT)
    grad_tokens = joined(
        d_x[:BLOCK], swap_bit(d_x[BLOCK:].astype(BF16), "tok", 0).astype(F32), half
    )

    mixed = jnp.stack(
        [grad_end_shift, grad_end_gain, grad_bias_outer, grad_mid_shift, grad_mid_gain]
    )
    small = jnp.concatenate(
        [mixed, grad_b_in.reshape(-1, width), jnp.zeros((3, width), F32)], axis=0
    )
    own_rows = grad_b_in.shape[0] // 2 // width
    theirs = mate(small)
    small = jnp.concatenate(
        [
            small[:5] + theirs[:5],
            small[5 : 5 + own_rows] + theirs[5 + own_rows : 5 + 2 * own_rows],
            jnp.zeros((1, width), F32),
        ],
        axis=0,
    )
    for bit in range(lax.axis_size("tok").bit_length() - 1):
        small = small + swap_bit(small, "tok", bit)

    cut = hidden // 2
    g_down = jnp.concatenate(tok_sum(g_down[:cut], g_down[cut:]), axis=0).astype(F32)
    cut = width // 2
    g_in = jnp.concatenate(tok_sum(g_in[:cut], g_in[cut:]), axis=0).astype(F32)
    g_qkv = jnp.concatenate(tok_sum(g_qkv[:cut], g_qkv[cut:]), axis=0).astype(F32)
    cut = own_out // 2
    g_out = jnp.concatenate(tok_sum(g_out[:cut], g_out[cut:]), axis=0).astype(F32)

    def unpack(at):
        return jnp.concatenate(
            [
                g_qkv[:, (3 * p + at) * LANES : (3 * p + at + 1) * LANES]
                for p in range(local_pairs)
            ],
            axis=1,
        )

    return (
        out,
        grad_tokens,
        unpack(0),
        unpack(1),
        unpack(2),
        g_out,
        small[4],
        small[3],
        g_in,
        small[5 : 5 + own_rows].reshape(-1),
        g_down,
        small[2],
        small[1],
        small[0],
    )


def solution(mesh):
    rows = P(("tok", "head"), None)
    return jax.shard_map(
        body,
        mesh=mesh,
        in_specs=(
            rows,
            rows,
            P(),
            P(),
            P(),
            P(None, "head"),
            P(None, "head"),
            P(None, "head"),
            P("head", None),
            P(),
            P(),
            P(None, "head"),
            P("head"),
            P("head", None),
            P(),
            P(),
            P(),
        ),
        out_specs=(
            rows,
            rows,
            P(None, "head"),
            P(None, "head"),
            P(None, "head"),
            P("head", None),
            P(),
            P(),
            P(None, "head"),
            P("head"),
            P("head", None),
            P(),
            P(),
            P(),
        ),
        check_vma=False,
    )
```

time: 1050 us -> 387 us (0.37)
  waiting for transfers between devices: 515 us -> 93.3 us
  matrix products: 290 us -> 98.5 us
  blocking collectives: 87.1 us -> 0 us
  starting transfers between devices: 5.44 us -> 67.5 us
  local copies, waits for them, and re-layouts: 93.7 us -> 39.8 us
  Pallas kernels: 0 us -> 36 us
  between operations: 14.8 us -> 2.44 us
    psum x1 -> x0, waiting for transfers between devices: 311 us -> none  [body(): lax.psum((grad_w_query, grad_w_key, grad_w_value, grad_w_output, grad_w_i...]
    dot_general x40 -> x16, matrix products: 290 us -> 98.5 us  [dot(): return lax.dot_general(a, b, (dims, ((), ())), preferred_element_type=F32)]
    psum x2 -> x0, blocking collectives: 87.1 us -> none  [the longest x1 45.6 us: body(): lax.psum((grad_w_query, grad_w_key, grad_w_value, grad_w_output, grad_w_i...]
    ppermute x4 -> x66, starting transfers between devices: 4.18 us -> 67.5 us  [swap_bit(): lax.ppermute(x, axis, [(i, i ^ 1 << bit) for i in range(lax.axis_size(axi...]
    all_gather x4 -> x0, waiting for transfers between devices: 52.1 us -> none  [the longest x1 13.4 us: body(): normed_all = lax.all_gather(normed_low, 'head', axis=0, tiled=True)]
    reduce_scatter x4 -> x0, waiting for transfers between devices: 37.9 us -> none  [the longest x1 15.5 us: body(): lax.psum_scatter(branch_terms, 'head', scatter_dimension=0, tiled=True)]
    pallas_call x0 -> x2, Pallas kernels: none -> 36 us  [the longest x1 21.2 us: attention_back(): pl.pallas_call(attend_back_kernel, grid=(pairs,), in_specs=[pl.BlockSpec(...]
    reshape x6 -> x2, local copies, waits for them, and re-layouts: 23.3 us -> 0.62 us  [the longest x1 0.61 us: body(): small[5:5 + own_rows].reshape(-1)]
  transfers between devices with their start and end apart: 13 -> 66, of which waited for: 12 -> 31; matrix products, arithmetic and copies ran while one was open for 6% -> 31% of each run, Pallas kernels for 0% -> 9%
where the time goes in v1:
time: 387 us; the launch traced here: 382 us
  matrix products  98.5 us (25%)
  waiting for transfers between devices  93.3 us (24%)
  starting transfers between devices  67.5 us (17%)
  other arithmetic  44.4 us (11%)
  local copies, waits for them, and re-layouts  39.8 us (10%)
  Pallas kernels  36 us (9%)
    dot_general x16, matrix products, dot(): return lax.dot_general(a, b, (dims, ((), ())), preferred_element_type=F32)  98.5 us
    ppermute x66, waiting for transfers between devices, swap_bit(): lax.ppermute(x, axis, [(i, i ^ 1 << bit) for i in range(lax.axis_size(axi...  93.3 us
    ppermute x66, starting transfers between devices, swap_bit(): lax.ppermute(x, axis, [(i, i ^ 1 << bit) for i in range(lax.axis_size(axi...  67.5 us
    pallas_call x1, Pallas kernels, attention_back(): pl.pallas_call(attend_back_kernel, grid=(pairs,), in_specs=[pl.BlockSpec(...  21.2 us
    unnamed x107, local copies, waits for them, and re-layouts  18.2 us
    pallas_call x1, Pallas kernels, attention(): pl.pallas_call(attend_kernel, grid=(pairs,), in_specs=[pl.BlockSpec((1, L...  14.8 us
    convert_element_type x1, other arithmetic, body(): d_u = d_u.astype(BF16)  11.5 us
  transfers between devices with their start and end apart: 66, of which 31 were waited for; matrix products, arithmetic and copies ran while one was open for 31% of the time, Pallas kernels for 9%

profile of v1, /device:TPU:0, one launch (start us, length us, event | category | flops | bytes accessed | tf_op | source)
XLA Modules:
  0.0 381.9 jit_solution(8206169888324205222)
XLA Ops:
  35.1 8.3 %convolution_convert_fusion.qkv_ref = bf16[1024,2304]{1,0:T(8,128)(2,1)} fusion(bf16[768,2304]{1,0:T(8,128)(2,1)} %constant_dynamic-update-slice_fusion, bf16[512,768]{1,0:T(8,128)(2,1)} %collective-permute-done, bf16[512,768]{1,0:T(8,128)(2,1)S(1)} %copy-done.20), kind=kOutput, calls=%fused_computation.8 | convolution fusion | flops 3629383680 | bytes 9830400 | tf_op jit(solution)/shard_map/dot_general | solution.py:28
  43.3 14.8 %attention_forward.1 = (bf16[1024,768]{1,0:T(8,128)(2,1)S(1)}, f32[6,2,1024]{2,1,0:T(2,128)S(1)}) custom-call(s32[1,768]{1,0:T(1,128)S(1)} %broadcast_in_dim_reshape.3.swap_ref, bf16[1024,2304]{1,0:T(8,128)(2,1)} %convolution_convert_fusion.qkv_ref), custom_call_target="tpu_custom_call" | custom-call | flops 6442450944 | bytes 6291456 | tf_op jit(solution)/shard_map/attention_forward/pallas_call | solution.py:109
  62.2 3.8 %constant_dynamic-update-slice_fusion.3 = bf16[768,3072]{1,0:T(8,128)(2,1)} fusion(bf16[768,3072]{1,0:T(8,128)(2,1)} %constant_dynamic-update-slice_fusion.4, bf16[768,1536]{1,0:T(8,128)(2,1)} %collective-permute-done.3), kind=kLoop, calls=%fused_computation.174 | loop fusion | bytes 4718592 | tf_op jit(solution)/shard_map/concatenate | solution.py:289
  66.0 16.6 %multiply_convert_fusion = (bf16[1024,3072]{1,0:T(8,128)(2,1)S(1)}, f32[1024,3072]{1,0:T(8,128)}) fusion(f32[3072]{0:T(1024)S(1)} %pad_maximum_fusion.37, bf16[1024,768]{1,0:T(8,128)(2,1)S(1)} %fusion.16, bf16[768,3072]{1,0:T(8,128)(2,1)} %constant_dynamic-update-slice_fusion.3), kind=kOutput, calls=%fused_computation.3 | convolution fusion | flops 4901044224 | bytes 25178112 | tf_op jit(solution)/shard_map/dot_general | solution.py:28
  83.4 5.4 %fusion.65 = (f32[1024]{0:T(1024)S(1)}, f32[1024,768]{1,0:T(8,128)S(1)}) fusion(f32[768]{0:T(1024)S(1)} %copy-done.33, bf16[1024,3072]{1,0:T(8,128)(2,1)S(1)} %get-tuple-element.101, bf16[3072,768]{1,0:T(8,128)(2,1)S(1)} %constant_dynamic-update-slice_fusion.5, f32[768]{0:T(1024)S(1)} %copy-done.29, f32[768]{0:T(1024)S(1)} %copy-done.27, ...), kind=kOutput, calls=%fused_computation.273 | convolution fusion | flops 4837342208 | bytes 17323008 | tf_op jit(solution)/shard_map/dot_general | solution.py:28
  95.3 4.1 %convolution_convert_fusion.1 = bf16[1536,768]{1,0:T(8,128)(2,1)} fusion(bf16[1024,3072]{1,0:T(8,128)(2,1)S(1)} %get-tuple-element.101, f32[1024,768]{1,0:T(8,128)S(1)} %get-tuple-element.34), kind=kOutput, calls=%fused_computation.12 | convolution fusion | flops 2417885184 | bytes 8650752 | tf_op jit(solution)/shard_map/dot_general | solution.py:28
  99.3 19.0 %fusion = (f32[3072]{0:T(1024)S(1)}, bf16[1024,3072]{1,0:T(8,128)(2,1)}, f32[1024,3072]{1,0:T(8,128)}) fusion(f32[1024,3072]{1,0:T(8,128)} %get-tuple-element.102, f32[3072]{0:T(1024)S(1)} %pad_maximum_fusion.37, bf16[3072,768]{1,0:T(8,128)(2,1)S(1)} %constant_dynamic-update-slice_fusion.5, f32[1024,768]{1,0:T(8,128)S(1)} %get-tuple-element.34), kind=kOutput, calls=%fused_computation.6 | convolution fusion | flops 4917556224 | bytes 39346176 | tf_op jit(solution)/shard_map/dot_general | solution.py:28
  118.3 11.5 %fusion.1 = bf16[1024,3072]{1,0:T(8,128)(2,1)} fusion(f32[1024,3072]{1,0:T(8,128)} %get-tuple-element.105, bf16[1024,3072]{1,0:T(8,128)(2,1)} %get-tuple-element.36), kind=kLoop, calls=%fused_computation.7 | loop fusion | flops 9437184 | bytes 25165824 | tf_op jit(solution)/shard_map/convert_element_type | solution.py:339
  129.8 5.9 %convolution_convert_fusion.2 = bf16[768,1536]{1,0:T(8,128)(2,1)} fusion(bf16[1024,768]{1,0:T(8,128)(2,1)S(1)} %copy-done.18, bf16[1024,3072]{1,0:T(8,128)(2,1)} %fusion.1), kind=kOutput, calls=%fused_computation.13 | convolution fusion | flops 2417098752 | bytes 7077888 | tf_op jit(solution)/shard_map/dot_general | solution.py:28
  136.0 9.8 %multiply_reduce_fusion = (f32[768]{0:T(1024)S(1)}, f32[1024]{0:T(1024)S(1)}, f32[1024]{0:T(1024)S(1)}, f32[768]{0:T(1024)S(1)}, f32[1024,768]{1,0:T(8,128)}) fusion(f32[1024,768]{1,0:T(8,128)S(1)} %copy-done.3, f32[1024]{0:T(1024)S(1)} %add_rsqrt_fusion.1, f32[1024]{0:T(1024)S(1)} %broadcast_multiply_fusion.5, f32[768]{0:T(1024)S(1)} %copy-done.27, ...), kind=kOutput, calls=%fused_computation.23 | convolution fusion | flops 4839698432 | bytes 20472832 | tf_op jit(solution)/shard_map/dot_general | solution.py:28
  156.2 21.2 %attention_backward.1 = bf16[1024,2304]{1,0:T(8,128)(2,1)} custom-call(s32[1,768]{1,0:T(1,128)S(1)} %broadcast_in_dim_reshape.3.swap_ref, bf16[1024,2304]{1,0:T(8,128)(2,1)} %convolution_convert_fusion.qkv_ref, bf16[1024,768]{1,0:T(8,128)(2,1)S(1)} %get-tuple-element.16.ctx_ref, bf16[1024,768]{1,0:T(8,128)(2,1)S(1)} %convolution_convert_fusion.4.dctx_ref, ...), custom_call_target="tpu_custom_call" | custom-call | flops 16106127360 | bytes 12582912 | tf_op jit(solution)/shard_map/attention_backward/pallas_call | solution.py:138
  180.5 5.9 %convolution_add_fusion.2 = f32[1024,768]{1,0:T(8,128)S(1)} fusion(f32[1024,768]{1,0:T(8,128)S(1)} %copy-done.5, bf16[1024,2304]{1,0:T(8,128)(2,1)S(1)} %copy-done.35, bf16[768,2304]{1,0:T(8,128)(2,1)} %constant_dynamic-update-slice_fusion), kind=kOutput, calls=%fused_computation.49 | convolution fusion | flops 3624665088 | bytes 14548992 | tf_op jit(solution)/shard_map/dot_general | solution.py:28
  191.1 4.6 %collective-permute-done.25 = bf16[96,768]{1,0:T(8,128)(2,1)S(1)} collective-permute-done((bf16[96,768]{1,0:T(8,128)(2,1)S(1)}, bf16[96,768]{1,0:T(8,128)(2,1)S(1)}, u32[]{:S(2)}, u32[]{:S(2)}) %collective-permute-start.25) | collective-permute-done | bytes 147488 | tf_op jit(solution)/shard_map/ppermute | solution.py:24
  196.3 3.8 collective-permute-done.24
  200.7 7.3 %collective-permute-done.26 = bf16[48,768]{1,0:T(8,128)(2,1)S(1)} collective-permute-done((bf16[48,768]{1,0:T(8,128)(2,1)S(1)}, bf16[48,768]{1,0:T(8,128)(2,1)S(1)}, u32[]{:S(2)}, u32[]{:S(2)}) %collective-permute-start.26) | collective-permute-done | bytes 73760 | tf_op jit(solution)/shard_map/ppermute | solution.py:24
  209.7 4.6 %convolution_convert_fusion.3 = bf16[768,1152]{1,0:T(8,128)(2,1)} fusion(bf16[1024,2304]{1,0:T(8,128)(2,1)S(1)} %copy-done.35, bf16[512,768]{1,0:T(8,128)(2,1)} %collective-permute-done, bf16[512,768]{1,0:T(8,128)(2,1)S(1)} %copy-done.22), kind=kOutput, calls=%fused_computation.15 | convolution fusion | flops 1815969792 | bytes 5701632 | tf_op jit(solution)/shard_map/dot_general | solution.py:28
  237.8 6.0 %collective-permute-done.6 = bf16[512,768]{1,0:T(8,128)(2,1)S(1)} collective-permute-done((bf16[512,768]{1,0:T(8,128)(2,1)}, bf16[512,768]{1,0:T(8,128)(2,1)S(1)}, u32[]{:S(2)}, u32[]{:S(2)}) %collective-permute-start.6) | collective-permute-done | bytes 786464 | tf_op jit(solution)/shard_map/ppermute | solution.py:24
  256.1 5.9 %collective-permute-done.10 = bf16[192,1152]{1,0:T(8,128)(2,1)S(1)} collective-permute-done((bf16[192,1152]{1,0:T(8,128)(2,1)S(1)}, bf16[192,1152]{1,0:T(8,128)(2,1)S(1)}, u32[]{:S(2)}, u32[]{:S(2)}) %collective-permute-start.10) | collective-permute-done | bytes 442400 | tf_op jit(solution)/shard_map/ppermute | solution.py:24
  267.6 4.5 %add_convert_fusion.1 = bf16[1536,768]{1,0:T(8,128)(2,1)S(1)} fusion(bf16[1536,768]{1,0:T(8,128)(2,1)} %collective-permute-done.53, bf16[1024,3072]{1,0:T(8,128)(2,1)S(1)} %bitcast.26, f32[1024,768]{1,0:T(8,128)S(1)} %copy-done.11), kind=kOutput, calls=%fused_computation.9 | convolution fusion | flops 2420244480 | bytes 11010048 | tf_op jit(solution)/shard_map/dot_general | solution.py:28
  274.6 4.2 %add_convert_fusion.2 = bf16[768,1536]{1,0:T(8,128)(2,1)S(1)} fusion(bf16[768,1536]{1,0:T(8,128)(2,1)} %collective-permute-done.40, bf16[1024,768]{1,0:T(8,128)(2,1)S(1)} %copy-done.19, bf16[1024,3072]{1,0:T(8,128)(2,1)S(1)} %bitcast.19), kind=kOutput, calls=%fused_computation.10 | convolution fusion | flops 2419458048 | bytes 9437184 | tf_op jit(solution)/shard_map/dot_general | solution.py:28
  279.7 5.4 %collective-permute-done.14 = bf16[96,1152]{1,0:T(8,128)(2,1)S(1)} collective-permute-done((bf16[96,1152]{1,0:T(8,128)(2,1)S(1)}, bf16[96,1152]{1,0:T(8,128)(2,1)S(1)}, u32[]{:S(2)}, u32[]{:S(2)}) %collective-permute-start.14) | collective-permute-done | bytes 221216 | tf_op jit(solution)/shard_map/ppermute | solution.py:24
  343.3 3.9 %collective-permute-done.61 = bf16[192,768]{1,0:T(8,128)(2,1)S(1)} collective-permute-done((bf16[192,768]{1,0:T(8,128)(2,1)S(1)}, bf16[192,768]{1,0:T(8,128)(2,1)S(1)}, u32[]{:S(2)}, u32[]{:S(2)}) %collective-permute-start.61) | collective-permute-done | bytes 294944 | tf_op jit(solution)/shard_map/ppermute | solution.py:24
  352.0 5.3 %collective-permute-done.62 = bf16[192,768]{1,0:T(8,128)(2,1)S(1)} collective-permute-done((bf16[192,768]{1,0:T(8,128)(2,1)S(1)}, bf16[192,768]{1,0:T(8,128)(2,1)S(1)}, u32[]{:S(2)}, u32[]{:S(2)}) %collective-permute-start.62) | collective-permute-done | bytes 294944 | tf_op jit(solution)/shard_map/ppermute | solution.py:24
  370.2 5.4 %collective-permute-done.50 = bf16[192,1536]{1,0:T(8,128)(2,1)S(1)} collective-permute-done((bf16[192,1536]{1,0:T(8,128)(2,1)S(1)}, bf16[192,1536]{1,0:T(8,128)(2,1)S(1)}, u32[]{:S(2)}, u32[]{:S(2)}) %collective-permute-start.50) | collective-permute-done | bytes 589856 | tf_op jit(solution)/shard_map/ppermute | solution.py:24
  (424 shorter events, 192.2 us)
Async XLA Ops:
  3.5 31.6 %collective-permute-start = (bf16[512,768]{1,0:T(8,128)(2,1)}, bf16[512,768]{1,0:T(8,128)(2,1)}, u32[]{:S(2)}, u32[]{:S(2)}) collective-permute-start(bf16[512,768]{1,0:T(8,128)(2,1)} %get-tuple-element.60), channel_id=1, source_target_pairs={{0,2},{2,0},{4,6},{6,4},{8,10},{10,8},{12,14},{14,12},{16,18},{18,... | collective-permute-start | bytes 2359304 | tf_op jit(solution)/shard_map/ppermute | solution.py:24
  12.9 19.3 %collective-permute-start.1 = (bf16[768,1152]{1,0:T(8,128)(2,1)}, bf16[768,1152]{1,0:T(8,128)(2,1)}, u32[]{:S(2)}, u32[]{:S(2)}) collective-permute-start(bf16[768,1152]{1,0:T(8,128)(2,1)} %get-tuple-element.63), channel_id=1, source_target_pairs={{0,1},{1,0},{2,3},{3,2},{4,5},{5,4},{6,7},{7,6},{8,9},{9,8},{10,11... | collective-permute-start | bytes 5308424 | tf_op jit(solution)/shard_map/ppermute | solution.py:24
  12.9 17.3 %collective-permute-start.2 = (bf16[384,768]{1,0:T(8,128)(2,1)}, bf16[384,768]{1,0:T(8,128)(2,1)}, u32[]{:S(2)}, u32[]{:S(2)}) collective-permute-start(bf16[384,768]{1,0:T(8,128)(2,1)} %param.25), channel_id=1, source_target_pairs={{0,1},{1,0},{2,3},{3,2},{4,5},{5,4},{6,7},{7,6},{8,9},{9,8},{10,11... | collective-permute-start | bytes 1769480 | tf_op jit(solution)/shard_map/ppermute | solution.py:24
  13.4 48.8 %collective-permute-start.3 = (bf16[768,1536]{1,0:T(8,128)(2,1)}, bf16[768,1536]{1,0:T(8,128)(2,1)}, u32[]{:S(2)}, u32[]{:S(2)}) collective-permute-start(bf16[768,1536]{1,0:T(8,128)(2,1)} %param.28), channel_id=1, source_target_pairs={{0,1},{1,0},{2,3},{3,2},{4,5},{5,4},{6,7},{7,6},{8,9},{9,8},{10,11... | collective-permute-start | bytes 7077896 | tf_op jit(solution)/shard_map/ppermute | solution.py:24
  13.4 16.7 %collective-permute-start.4 = (f32[1536]{0:T(1024)S(1)}, f32[1536]{0:T(1024)S(1)}, u32[]{:S(2)}, u32[]{:S(2)}) collective-permute-start(f32[1536]{0:T(1024)S(1)} %copy-done.28), channel_id=1, source_target_pairs={{0,1},{1,0},{2,3},{3,2},{4,5},{5,4},{6,7},{7,6},{8,9},{9,8},{10,11... | collective-permute-start | bytes 18440 | tf_op jit(solution)/shard_map/ppermute | solution.py:24
  30.2 52.6 %collective-permute-start.5 = (bf16[1536,768]{1,0:T(8,128)(2,1)}, bf16[1536,768]{1,0:T(8,128)(2,1)S(1)}, u32[]{:S(2)}, u32[]{:S(2)}) collective-permute-start(bf16[1536,768]{1,0:T(8,128)(2,1)} %param.30), channel_id=1, source_target_pairs={{0,1},{1,0},{2,3},{3,2},{4,5},{5,4},{6,7},{7,6},{8,9},{9,8},{10,11... | collective-permute-start | bytes 7077896 | tf_op jit(solution)/shard_map/ppermute | solution.py:24
  30.2 59.2 %collective-permute-start.7 = (bf16[512,768]{1,0:T(8,128)(2,1)}, bf16[512,768]{1,0:T(8,128)(2,1)S(1)}, u32[]{:S(2)}, u32[]{:S(2)}) collective-permute-start(bf16[512,768]{1,0:T(8,128)(2,1)} %get-tuple-element.56), channel_id=1, source_target_pairs={{0,2},{2,0},{4,6},{6,4},{8,10},{10,8},{12,14},{14,12},{16,18},{18,... | collective-permute-start | bytes 2359304 | tf_op jit(solution)/shard_map/ppermute | solution.py:24
  153.4 114.1 %collective-permute-start.53 = (bf16[1536,768]{1,0:T(8,128)(2,1)}, bf16[1536,768]{1,0:T(8,128)(2,1)}, u32[]{:S(2)}, u32[]{:S(2)}) collective-permute-start(bf16[1536,768]{1,0:T(8,128)(2,1)} %convolution_convert_fusion.1), channel_id=1, source_target_pairs={{0,1},{1,0},{2,3},{3,2},{4,5},{5,4},{6,7},{7,6},{8,9},{9,8},{10,11... | collective-permute-start | bytes 7077896 | tf_op jit(solution)/shard_map/ppermute | solution.py:24
  153.6 121.0 %collective-permute-start.40 = (bf16[768,1536]{1,0:T(8,128)(2,1)}, bf16[768,1536]{1,0:T(8,128)(2,1)}, u32[]{:S(2)}, u32[]{:S(2)}) collective-permute-start(bf16[768,1536]{1,0:T(8,128)(2,1)} %convolution_convert_fusion.2), channel_id=1, source_target_pairs={{0,1},{1,0},{2,3},{3,2},{4,5},{5,4},{6,7},{7,6},{8,9},{9,8},{10,11... | collective-permute-start | bytes 7077896 | tf_op jit(solution)/shard_map/ppermute | solution.py:24
  154.0 24.9 %collective-permute-start.22 = (bf16[384,768]{1,0:T(8,128)(2,1)}, bf16[384,768]{1,0:T(8,128)(2,1)S(1)}, u32[]{:S(2)}, u32[]{:S(2)}) collective-permute-start(bf16[384,768]{1,0:T(8,128)(2,1)} %convolution_convert_fusion.5), channel_id=1, source_target_pairs={{0,1},{1,0},{2,3},{3,2},{4,5},{5,4},{6,7},{7,6},{8,9},{9,8},{10,11... | collective-permute-start | bytes 1769480 | tf_op jit(solution)/shard_map/ppermute | solution.py:24
  154.2 23.1 %collective-permute-start.36 = (f32[8,768]{1,0:T(8,128)S(1)}, f32[8,768]{1,0:T(8,128)S(1)}, u32[]{:S(2)}, u32[]{:S(2)}) collective-permute-start(f32[8,768]{1,0:T(8,128)S(1)} %maximum_maximum_fusion), channel_id=1, source_target_pairs={{0,2},{2,0},{4,6},{6,4},{8,10},{10,8},{12,14},{14,12},{16,18},{18,... | collective-permute-start | bytes 73736 | tf_op jit(solution)/shard_map/ppermute | solution.py:24
  187.3 36.4 %collective-permute-start.8 = (bf16[512,768]{1,0:T(8,128)(2,1)}, bf16[512,768]{1,0:T(8,128)(2,1)}, u32[]{:S(2)}, u32[]{:S(2)}) collective-permute-start(bf16[512,768]{1,0:T(8,128)(2,1)} %slice.465), channel_id=1, source_target_pairs={{0,2},{2,0},{4,6},{6,4},{8,10},{10,8},{12,14},{14,12},{16,18},{18,... | collective-permute-start | bytes 2359304 | tf_op jit(solution)/shard_map/ppermute | solution.py:24
  188.9 25.5 %collective-permute-start.38 = (f32[8,768]{1,0:T(8,128)S(1)}, f32[8,768]{1,0:T(8,128)S(1)}, u32[]{:S(2)}, u32[]{:S(2)}) collective-permute-start(f32[8,768]{1,0:T(8,128)S(1)} %add.467), channel_id=1, source_target_pairs={{0,8},{2,10},{4,12},{6,14},{8,0},{10,2},{12,4},{14,6},{16,24},{18,... | collective-permute-start | bytes 73736 | tf_op jit(solution)/shard_map/ppermute | solution.py:24
  219.9 29.1 %collective-permute-start.9 = (bf16[768,1152]{1,0:T(8,128)(2,1)}, bf16[768,1152]{1,0:T(8,128)(2,1)S(1)}, u32[]{:S(2)}, u32[]{:S(2)}) collective-permute-start(bf16[768,1152]{1,0:T(8,128)(2,1)} %convolution_convert_fusion.3), channel_id=1, source_target_pairs={{0,1},{1,0},{2,3},{3,2},{4,5},{5,4},{6,7},{7,6},{8,9},{9,8},{10,11... | collective-permute-start | bytes 5308424 | tf_op jit(solution)/shard_map/ppermute | solution.py:24
  223.7 20.1 %collective-permute-start.6 = (bf16[512,768]{1,0:T(8,128)(2,1)}, bf16[512,768]{1,0:T(8,128)(2,1)S(1)}, u32[]{:S(2)}, u32[]{:S(2)}) collective-permute-start(bf16[512,768]{1,0:T(8,128)(2,1)} %get-tuple-element.58), channel_id=1, source_target_pairs={{0,2},{2,0},{4,6},{6,4},{8,10},{10,8},{12,14},{14,12},{16,18},{18,... | collective-permute-start | bytes 2359304 | tf_op jit(solution)/shard_map/ppermute | solution.py:24
  262.1 16.7 %collective-permute-start.11 = (bf16[96,1152]{1,0:T(8,128)(2,1)S(1)}, bf16[96,1152]{1,0:T(8,128)(2,1)S(1)}, u32[]{:S(2)}, u32[]{:S(2)}) collective-permute-start(bf16[96,1152]{1,0:T(8,128)(2,1)S(1)} %constant_dynamic-slice_fusion.30), channel_id=1, source_target_pairs={{0,4},{2,6},{4,0},{6,2},{8,12},{10,14},{12,8},{14,10},{16,20},{18,... | collective-permute-start | bytes 663560 | tf_op jit(solution)/shard_map/ppermute | solution.py:24
  272.4 26.5 %collective-permute-start.54 = (bf16[384,768]{1,0:T(8,128)(2,1)S(1)}, bf16[384,768]{1,0:T(8,128)(2,1)S(1)}, u32[]{:S(2)}, u32[]{:S(2)}) collective-permute-start(bf16[384,768]{1,0:T(8,128)(2,1)S(1)} %constant_dynamic-slice_fusion.7), channel_id=1, source_target_pairs={{0,2},{2,0},{4,6},{6,4},{8,10},{10,8},{12,14},{14,12},{16,18},{18,... | collective-permute-start | bytes 1769480 | tf_op jit(solution)/shard_map/ppermute | solution.py:24
  274.0 26.7 %collective-permute-start.56 = (bf16[384,768]{1,0:T(8,128)(2,1)S(1)}, bf16[384,768]{1,0:T(8,128)(2,1)S(1)}, u32[]{:S(2)}, u32[]{:S(2)}) collective-permute-start(bf16[384,768]{1,0:T(8,128)(2,1)S(1)} %constant_dynamic-slice_fusion.4), channel_id=1, source_target_pairs={{0,4},{2,6},{4,0},{6,2},{8,12},{10,14},{12,8},{14,10},{16,20},{18,... | collective-permute-start | bytes 1769480 | tf_op jit(solution)/shard_map/ppermute | solution.py:24
  286.9 15.2 %collective-permute-start.41 = (bf16[192,1536]{1,0:T(8,128)(2,1)S(1)}, bf16[192,1536]{1,0:T(8,128)(2,1)S(1)}, u32[]{:S(2)}, u32[]{:S(2)}) collective-permute-start(bf16[192,1536]{1,0:T(8,128)(2,1)S(1)} %constant_dynamic-slice_fusion.15), channel_id=1, source_target_pairs={{0,2},{2,0},{4,6},{6,4},{8,10},{10,8},{12,14},{14,12},{16,18},{18,... | collective-permute-start | bytes 1769480 | tf_op jit(solution)/shard_map/ppermute | solution.py:24
  302.3 13.7 %collective-permute-start.42 = (bf16[96,1536]{1,0:T(8,128)(2,1)S(1)}, bf16[96,1536]{1,0:T(8,128)(2,1)S(1)}, u32[]{:S(2)}, u32[]{:S(2)}) collective-permute-start(bf16[96,1536]{1,0:T(8,128)(2,1)S(1)} %constant_dynamic-slice_fusion.14), channel_id=1, source_target_pairs={{0,4},{2,6},{4,0},{6,2},{8,12},{10,14},{12,8},{14,10},{16,20},{18,... | collective-permute-start | bytes 884744 | tf_op jit(solution)/shard_map/ppermute | solution.py:24
  320.3 16.7 %collective-permute-start.19 = (bf16[192,1152]{1,0:T(8,128)(2,1)S(1)}, bf16[192,1152]{1,0:T(8,128)(2,1)S(1)}, u32[]{:S(2)}, u32[]{:S(2)}) collective-permute-start(bf16[192,1152]{1,0:T(8,128)(2,1)S(1)} %maximum_select_fusion.12), channel_id=1, source_target_pairs={{0,2},{2,0},{4,6},{6,4},{8,10},{10,8},{12,14},{14,12},{16,18},{18,... | collective-permute-start | bytes 1327112 | tf_op jit(solution)/shard_map/ppermute | solution.py:24
  321.2 16.0 %collective-permute-start.21 = (bf16[192,1152]{1,0:T(8,128)(2,1)S(1)}, bf16[192,1152]{1,0:T(8,128)(2,1)S(1)}, u32[]{:S(2)}, u32[]{:S(2)}) collective-permute-start(bf16[192,1152]{1,0:T(8,128)(2,1)S(1)} %maximum_select_fusion.13), channel_id=1, source_target_pairs={{0,4},{2,6},{4,0},{6,2},{8,12},{10,14},{12,8},{14,10},{16,20},{18,... | collective-permute-start | bytes 1327112 | tf_op jit(solution)/shard_map/ppermute | solution.py:24
  351.3 13.8 %collective-permute-start.51 = (bf16[96,1536]{1,0:T(8,128)(2,1)S(1)}, bf16[96,1536]{1,0:T(8,128)(2,1)S(1)}, u32[]{:S(2)}, u32[]{:S(2)}) collective-permute-start(bf16[96,1536]{1,0:T(8,128)(2,1)S(1)} %fusion.27), channel_id=1, source_target_pairs={{0,2},{2,0},{4,6},{6,4},{8,10},{10,8},{12,14},{14,12},{16,18},{18,... | collective-permute-start | bytes 884744 | tf_op jit(solution)/shard_map/ppermute | solution.py:24
  361.8 13.7 %collective-permute-start.50 = (bf16[192,1536]{1,0:T(8,128)(2,1)S(1)}, bf16[192,1536]{1,0:T(8,128)(2,1)S(1)}, u32[]{:S(2)}, u32[]{:S(2)}) collective-permute-start(bf16[192,1536]{1,0:T(8,128)(2,1)S(1)} %maximum_select_fusion.8), channel_id=1, source_target_pairs={{0,2},{2,0},{4,6},{6,4},{8,10},{10,8},{12,14},{14,12},{16,18},{18,... | collective-permute-start | bytes 1769480 | tf_op jit(solution)/shard_map/ppermute | solution.py:24
  (88 other events, 892.0 us)
